TPU v7x, 32 devices: a whole 2x2x4 slice. The times are simulated.
32 devices in a mesh: ctx: 16 (over z, x, core), head: 2 (over y).
Axes of the slice: x: 2, y: 2, z: 4, core: 2. Of those that a mesh axis runs over, the one named last changes fastest.
Arguments:
- queries: bfloat16 [2048, 1536], P('ctx', 'head'), may hold values from -6 to 6
- key_states: bfloat16 [2048, 256], P('ctx', 'head'), may hold values from -8 to 8
- value_states: bfloat16 [2048, 256], P('ctx', 'head'), may hold values from -6 to 6
- out_grad: bfloat16 [2048, 1536], P('ctx', 'head'), may hold values from -6 to 6
- norm_gain: float32 [1536], P('head'), may hold values from 0.1 to 1.9
- mask_kind: int32 [4], replicated, may hold values from 0 to 1
- range_start: int32 [4], replicated, may hold values from 0 to 3, as said below
- placement: int32 [4], replicated, may hold values from 0 to 3, each once
Outputs:
- attn_out: bfloat16 [2048, 1536], P('ctx', 'head')
- d_queries: bfloat16 [2048, 1536], P('ctx', 'head')
- d_keys: bfloat16 [2048, 256], P('ctx', 'head')
- d_values: bfloat16 [2048, 256], P('ctx', 'head')
Inputs may be any that keep to these rules, and one draw needn't show every extreme that they name: range_start[i] <= i for every span i; the last span sees no earlier span. `placement`: every span number appears in exactly one slot.
All inputs are finite; a program needn't handle non-finite values.
Results may differ from a plain program's by a relative error of at most 0.04.
Values may be sent and summed in bfloat16 or wider, within the bound.
A program may use at most 64 MiB of HBM per device.

v0:
```python
import functools
import math

import jax
import jax.numpy as jnp
from jax import lax
from jax.experimental import pallas as pl
from jax.experimental.pallas import tpu as pltpu
from jax.sharding import PartitionSpec as P

MESH = pl.DeviceIdType.MESH
NEG = -1e30
EPS = 1e-06
HIDDEN = 1 << 30
F32 = jnp.float32
BF16 = jnp.bfloat16


def fold_rows(op, tile):
    return op(tile.reshape(tile.shape[0] // 8, 8, tile.shape[1]), axis=0)


def kernel(
    nz, nh, span_len, q_hbm, k_hbm, v_hbm, g_hbm, gain_hbm, kind_hbm, start_hbm, place_hbm,
    o_hbm, dq_hbm, dk_hbm, dv_hbm,
    q_ref, g_ref, gain_ref, kind_ref, start_ref, place_ref, o_ref, dq_ref, dk_ref, dv_ref, in_sems, out_sems,
    kv, scores, d_probs, tops, k_cols, row_max, row_sum, acc, q_rows, q_cols, g_rows, g_cols, stat, stat_in,
    mine, core_out, core_in, x_out, x_in, z_out, z_in,
    kv_recv, zs_send, xs_send, cs_send, stat_send, stat_recv,
    rc_send, rc_recv, rx_send, rx_recv, rz_send, rz_recv,
):
    tok, width = q_ref.shape
    dim = k_hbm.shape[1]
    heads = width // dim
    pair = 2 * tok
    steps = 2 * nz
    inv_sqrt = 1.0 / math.sqrt(dim)
    scale = inv_sqrt * math.log2(math.e)
    me, hd = lax.axis_index("ctx"), lax.axis_index("head")
    core, x, z = lax.rem(me, 2), lax.rem(me // 2, 2), me // 4
    cols = [slice(h * dim, (h + 1) * dim) for h in range(heads)]
    size = 2 if heads % 2 == 0 else 1
    groups = [range(h, h + size) for h in range(0, heads, size)]

    def span_of(group):
        return slice(group[0] * dim, (group[-1] + 1) * dim)


    def at(zz, xx, cc):
        return (zz * 2 + xx) * 2 + cc

    x_peer, core_peer = at(z, 1 - x, core), at(z, x, 1 - core)

    barrier = pltpu.get_barrier_semaphore()
    for k in range(1, nz):
        pl.semaphore_signal(barrier, inc=1, device_id=(at(lax.rem(z + k, nz), x, core), hd), device_id_type=MESH)
    pl.semaphore_signal(barrier, inc=1, device_id=(x_peer, hd), device_id_type=MESH)
    pl.semaphore_signal(barrier, inc=1, device_id=(core_peer, hd), device_id_type=MESH)
    for k in range(1, nh):
        pl.semaphore_signal(barrier, inc=1, device_id=(me, lax.rem(hd + k, nh)), device_id_type=MESH)

    moves = [
        pltpu.make_async_copy(src, dst, in_sems.at[n])
        for n, (src, dst) in enumerate((
            (k_hbm, kv.at[me, 0]), (v_hbm, kv.at[me, 1]), (q_hbm, q_ref), (g_hbm, g_ref), (gain_hbm, gain_ref),
            (kind_hbm, kind_ref), (start_hbm, start_ref), (place_hbm, place_ref),
        ))
    ]
    for move in moves:
        move.start()
    for move in moves[:3]:
        move.wait()
    squares = jnp.zeros((tok, dim), F32)
    for c in cols:
        part = q_ref[:, c].astype(F32)
        squares += part * part
    own_sum = jnp.sum(squares.T, axis=0, keepdims=True)
    stat[...] = jnp.broadcast_to(own_sum, stat.shape)
    pl.semaphore_wait(barrier, nz + nh)

    def remote(src, dst, send, recv, ctx_to, head_to=None):
        return pltpu.make_async_remote_copy(
            src_ref=src, dst_ref=dst, send_sem=send, recv_sem=recv,
            device_id=(ctx_to, hd if head_to is None else head_to), device_id_type=MESH,
        )

    def stat_copy(k):
        return remote(stat, stat_in.at[k - 1], stat_send.at[k - 1], stat_recv.at[k - 1], me, lax.rem(hd + k, nh))

    def kv_copy(block, send, to):
        return remote(kv.at[block], kv.at[block], send, kv_recv.at[block], to)

    def z_copy(k):
        return kv_copy(me, zs_send.at[k - 1], at(lax.rem(z + k, nz), x, core))

    for k in range(1, nh):
        stat_copy(k).start()
    kv_copy(me, cs_send.at[0], core_peer).start()
    kv_copy(me, xs_send.at[0], x_peer).start()
    for k in range(1, nz):
        z_copy(k).start()

    for move in moves[3:]:
        move.wait()
    for h, c in enumerate(cols):
        piece = g_ref[:, c]
        g_rows[h * tok:(h + 1) * tok, :] = piece
        g_cols[:, c] = piece.astype(F32).T.astype(BF16)
    row_max[...] = jnp.full(row_max.shape, NEG, F32)
    row_sum[...] = jnp.zeros(row_sum.shape, F32)
    acc[...] = jnp.zeros(acc.shape, F32)
    total = own_sum
    for k in range(1, nh):
        stat_copy(k).wait_recv()
        total = total + stat_in[k - 1, 0:1, :]
    inv_row = lax.rsqrt(total / (width * nh) + EPS)
    inv_col = jnp.broadcast_to(inv_row, (dim, tok)).T
    for h, c in enumerate(cols):
        normed = q_ref[:, c].astype(F32) * inv_col * gain_ref[c].reshape(1, dim)
        normed = normed.astype(BF16)
        q_rows[h * tok:(h + 1) * tok, :] = normed
        q_cols[:, c] = normed.astype(F32).T.astype(BF16)

    slot = (me * tok) // span_len
    q_span = place_ref[slot]
    lower = start_ref[q_span]
    causal = kind_ref[q_span]
    q_pos = lax.rem(me * tok, span_len) + lax.broadcasted_iota(jnp.int32, (1, tok), 1)

    def place_of(i):
        return lax.rem(z + i, nz), lax.rem(x + i // nz, 2)

    def pair_of(i):
        zz, xx = place_of(i)
        return zz * 2 + xx

    def keys_of(j):
        return kv[pl.ds(2 * j, 2), 0].reshape(pair, dim)

    def values_of(j):
        return kv[pl.ds(2 * j, 2), 1].reshape(pair, dim)

    def score_step(i, carry):
        @pl.when((i > 0) & (i < steps))
        def _():
            zz, xx = place_of(i)
            block = at(zz, xx, core)
            kv_copy(block, cs_send.at[i], core_peer).wait_recv()
            kv_copy(block, cs_send.at[i], core_peer).start()

            @pl.when(i < nz)
            def _():
                kv_copy(block, xs_send.at[i], x_peer).start()

        @pl.when(i > 0)
        def _():
            zz, xx = place_of(i - 1)
            j = zz * 2 + xx
            other = at(zz, xx, 1 - core)
            kv_copy(other, cs_send.at[0], core_peer).wait_recv()
            k_slot = (j * pair) // span_len
            k_span = place_ref[k_slot]
            before = (lower <= k_span) & (k_span < q_span)
            own = k_slot == slot
            stride = jnp.where(own & (causal != 0), 1, 0)
            offset = jnp.where(own | before, jnp.where(stride == 1, 0, -1), HIDDEN)
            k_pos = lax.rem(j * pair, span_len) + lax.broadcasted_iota(jnp.int32, (pair, tok), 0)
            allowed = k_pos * stride + offset <= q_pos
            bias = jnp.where(allowed, 0.0, NEG)
            keys, values = keys_of(j), values_of(j)
            value_cols = values.T
            k_cols[j] = keys.T
            for group in groups:
                wide = span_of(group)
                tile = jnp.dot(keys, q_cols[:, wide], preferred_element_type=F32)
                d_prob = jnp.dot(values, g_cols[:, wide], preferred_element_type=F32)
                d_probs[j, :, wide] = d_prob * inv_sqrt
                weights = []
                for n, h in enumerate(group):
                    c = cols[h]
                    part = tile[:, cols[n]] * scale + bias
                    old = row_max[0:1, c]
                    new = jnp.maximum(old, jnp.max(fold_rows(jnp.max, part), axis=0, keepdims=True))
                    weight = jnp.exp2(part - new)
                    scores[j, :, c] = weight
                    factor = jnp.exp2(old - new)
                    row_max[0:1, c] = new
                    tops[j, 0:1, c] = new
                    row_sum[:, c] = row_sum[:, c] * factor + fold_rows(jnp.sum, weight)
                    acc[:, c] = acc[:, c] * factor
                    weights.append(weight.astype(BF16))
                acc[:, wide] += jnp.dot(value_cols, jnp.concatenate(weights, axis=1), preferred_element_type=F32)

        return carry

    lax.fori_loop(0, steps + 1, score_step, 0)

    sums = jnp.sum(row_sum[...], axis=0, keepdims=True)
    log_sum = row_max[0:1, :] + jnp.log2(sums)
    deltas = []
    for c in cols:
        out = (acc[:, c] / sums[:, c]).astype(BF16).astype(F32)
        deltas.append(jnp.sum(out * g_cols[:, c].astype(F32), axis=0, keepdims=True) * inv_sqrt)
        o_ref[:, c] = out.T.astype(BF16)
    leave = [
        pltpu.make_async_copy(src, dst, out_sems.at[n])
        for n, (src, dst) in enumerate(((o_ref, o_hbm), (dq_ref, dq_hbm), (dk_ref, dk_hbm), (dv_ref, dv_hbm)))
    ]
    leave[0].start()
    acc[...] = jnp.zeros(acc.shape, F32)

    def core_copy(i):
        return remote(core_out.at[i], core_in.at[i], rc_send.at[i], rc_recv.at[i], core_peer)

    def x_copy(i):
        return remote(x_out.at[i], x_in.at[i], rx_send.at[i], rx_recv.at[i], x_peer)

    def rz_copy(i):
        return remote(z_out.at[i], z_in.at[i], rz_send.at[i], rz_recv.at[i], at(lax.rem(z + 1 + i, nz), x, core))

    def both_cores(i):
        core_copy(i).wait_recv()
        return mine[i] + core_in[i].astype(F32)

    def both_x(i):
        x_copy(i).wait_recv()
        return both_cores(nz + i) + x_in[i].astype(F32)

    def backward_step(i, carry):
        zz = lax.rem(z + 1 + i, nz)
        xx = lax.rem(x + 1 + i // nz, 2)
        j = zz * 2 + xx
        ratio = jnp.exp2(tops[j, 0:1, :] - log_sum)
        d_key = jnp.zeros((pair, dim), F32)
        d_value = jnp.zeros((pair, dim), F32)
        for group in groups:
            wide = span_of(group)
            tall = slice(group[0] * tok, (group[-1] + 1) * tok)
            probs, d_scores = [], []
            for h in group:
                c = cols[h]
                prob = scores[j, :, c] * ratio[:, c]
                probs.append(prob.astype(BF16))
                d_scores.append((prob * (d_probs[j, :, c] - deltas[h])).astype(BF16))
            d_score = jnp.concatenate(d_scores, axis=1)
            acc[:, wide] += jnp.dot(k_cols[j], d_score, preferred_element_type=F32)
            d_key += jnp.dot(d_score, q_rows[tall, :], preferred_element_type=F32)
            d_value += jnp.dot(jnp.concatenate(probs, axis=1), g_rows[tall, :], preferred_element_type=F32)
        first = core == 0
        for n, grad in enumerate((d_key, d_value)):
            low, high = grad[:tok], grad[tok:]
            mine[i, n] = jnp.where(first, low, high)
            core_out[i, n] = jnp.where(first, high, low).astype(BF16)
        core_copy(i).start()

        @pl.when((i >= 1) & (i <= nz))
        def _():
            x_out[i - 1] = both_cores(i - 1).astype(BF16)
            x_copy(i - 1).start()

        @pl.when(i > nz)
        def _():
            n = i - 1 - nz
            z_out[n] = both_x(n).astype(BF16)
            rz_copy(n).start()

        return carry

    lax.fori_loop(0, steps, backward_step, 0)

    for c in cols:
        dq_ref[:, c] = acc[:, c].T.astype(BF16)
    leave[1].start()
    grads = both_x(nz - 1)
    for n in range(nz - 1):
        rz_copy(n).wait_recv()
        grads = grads + z_in[n].astype(F32)
    dk_ref[...] = grads[0].astype(BF16)
    dv_ref[...] = grads[1].astype(BF16)
    leave[2].start()
    leave[3].start()

    for k in range(1, nh):
        stat_copy(k).wait_send()
    for k in range(1, nz):
        z_copy(k).wait_send()
        rz_copy(k - 1).wait_send()
    for i in range(nz):
        kv_copy(me, xs_send.at[i], x_peer).wait_send()
        x_copy(i).wait_send()
    for i in range(steps):
        kv_copy(me, cs_send.at[i], core_peer).wait_send()
        core_copy(i).wait_send()
    for move in leave:
        move.wait()


def hand_over(*refs):
    count = (len(refs) - 2) // 3
    given, taken, held = refs[:count], refs[count:2 * count], refs[2 * count:3 * count]
    in_sems, out_sems = refs[3 * count:]
    loads = [pltpu.make_async_copy(given[n], held[n], in_sems.at[n]) for n in range(count)]
    stores = [pltpu.make_async_copy(held[n], taken[n], out_sems.at[n]) for n in range(count)]
    for load in loads:
        load.start()
    for load, store in zip(loads, stores):
        load.wait()
        store.start()
    for store in stores:
        store.wait()


def solution(mesh):
    ranks, nh = mesh.shape["ctx"], mesh.shape["head"]
    nz = ranks // 4

    def shards(queries, key_states, value_states, out_grad, norm_gain, mask_kind, range_start, placement):
        tok, width = queries.shape
        dim = key_states.shape[1]
        heads = width // dim
        span_len = ranks * tok // placement.shape[0]
        steps = 2 * nz
        block = (2, tok, dim)
        anywhere = pl.BlockSpec(memory_space=pl.ANY)
        spans = placement.shape
        dma = pltpu.SemaphoreType.DMA
        rows = heads * tok
        out_shape = (
            jax.ShapeDtypeStruct(queries.shape, BF16),
            jax.ShapeDtypeStruct(queries.shape, BF16),
            jax.ShapeDtypeStruct(key_states.shape, BF16),
            jax.ShapeDtypeStruct(value_states.shape, BF16),
        )
        results = pl.pallas_call(
            functools.partial(kernel, nz, nh, span_len),
            out_shape=out_shape,
            in_specs=[anywhere] * 8,
            out_specs=(anywhere,) * 4,
            scratch_shapes=[
                pltpu.VMEM(queries.shape, BF16),
                pltpu.VMEM(queries.shape, BF16),
                pltpu.VMEM(norm_gain.shape, F32),
                pltpu.SMEM(spans, jnp.int32),
                pltpu.SMEM(spans, jnp.int32),
                pltpu.SMEM(spans, jnp.int32),
                pltpu.VMEM(queries.shape, BF16),
                pltpu.VMEM(queries.shape, BF16),
                pltpu.VMEM((tok, dim), BF16),
                pltpu.VMEM((tok, dim), BF16),
                dma((8,)), dma((4,)),
                pltpu.VMEM((ranks,) + block, BF16),
                pltpu.VMEM((steps, 2 * tok, rows), F32),
                pltpu.VMEM((steps, 2 * tok, rows), F32),
                pltpu.VMEM((steps, 8, rows), F32),
                pltpu.VMEM((steps, dim, 2 * tok), BF16),
                pltpu.VMEM((8, rows), F32),
                pltpu.VMEM((8, rows), F32),
                pltpu.VMEM((dim, rows), F32),
                pltpu.VMEM((rows, dim), BF16),
                pltpu.VMEM((dim, rows), BF16),
                pltpu.VMEM((rows, dim), BF16),
                pltpu.VMEM((dim, rows), BF16),
                pltpu.VMEM((8, tok), F32),
                pltpu.VMEM((nh - 1, 8, tok), F32),
                pltpu.VMEM((steps,) + block, F32),
                pltpu.VMEM((steps,) + block, BF16),
                pltpu.VMEM((steps,) + block, BF16),
                pltpu.VMEM((nz,) + block, BF16),
                pltpu.VMEM((nz,) + block, BF16),
                pltpu.VMEM((nz - 1,) + block, BF16),
                pltpu.VMEM((nz - 1,) + block, BF16),
                dma((ranks,)), dma((nz - 1,)), dma((nz,)), dma((steps,)),
                dma((nh - 1,)), dma((nh - 1,)),
                dma((steps,)), dma((steps,)),
                dma((nz,)), dma((nz,)),
                dma((nz - 1,)), dma((nz - 1,)),
            ],
            compiler_params=pltpu.CompilerParams(
                collective_id=0, has_side_effects=True, vmem_limit_bytes=56 * 1024 * 1024
            ),
        )(
            queries, key_states, value_states, out_grad, norm_gain, mask_kind, range_start, placement
        )
        return pl.pallas_call(
            hand_over,
            out_shape=out_shape,
            in_specs=[anywhere] * 4,
            out_specs=(anywhere,) * 4,
            scratch_shapes=[pltpu.VMEM(leaf.shape, BF16) for leaf in out_shape] + [dma((4,)), dma((4,))],
            compiler_params=pltpu.CompilerParams(vmem_limit_bytes=60 * 1024 * 1024),
        )(*results)

    tokens = P("ctx", "head")
    return jax.shard_map(
        shards,
        mesh=mesh,
        in_specs=(tokens,) * 4 + (P("head"), P(), P(), P()),
        out_specs=(tokens,) * 4,
        check_vma=False,
    )
```

profile of v0, /device:TPU:0, one launch (start us, length us, event | category | flops | bytes accessed | tf_op | source)
XLA Modules:
  0.0 35.3 jit_solution(9965497919972551595)
XLA Ops:
  0.6 32.9 %shard_map.111 = (bf16[128,768]{1,0:T(8,128)(2,1)}, bf16[128,768]{1,0:T(8,128)(2,1)}, bf16[128,128]{1,0:T(8,128)(2,1)}, bf16[128,128]{1,0:T(8,128)(2,1)}) custom-call(bf16[128,768]{1,0:T(8,128)(2,1)} %q_hbm.1, bf16[128,128]{1,0:T(8,128)(2,1)} %k_hbm.1, bf16[128,128]{1,0:T(8,128)(2,1)} %v_hbm.1, bf16[128,768]{1,0:T(8,128)(2,1)} %g_hbm.1, f32[768]{0:T(1024)} %gain_hbm.1, ...), custom_call_target="tpu_custom_call" | custom-call | tf_op jit(solution)/shard_map/pallas_call | solution.py:334
  33.5 1.8 %shard_map.112 = (bf16[128,768]{1,0:T(8,128)(2,1)}, bf16[128,768]{1,0:T(8,128)(2,1)}, bf16[128,128]{1,0:T(8,128)(2,1)}, bf16[128,128]{1,0:T(8,128)(2,1)}) custom-call(bf16[128,768]{1,0:T(8,128)(2,1)} %get-tuple-element.8.refs_0_, bf16[128,768]{1,0:T(8,128)(2,1)} %get-tuple-element.9.refs_1_, bf16[128,128]{1,0:T(8,128)(2,1)} %get-tuple-element.10.refs_2_, ...), custom_call_target="tpu_custom_call" | custom-call | tf_op jit(solution)/shard_map/pallas_call | solution.py:384
where the time goes:
time: 35.4 us; the launch traced here: 35.3 us
  Pallas kernels  34.7 us (98%)
  between operations  0.64 us (2%)
    pallas_call x1, Pallas kernels, shards(): pl.pallas_call(functools.partial(kernel, nz, nh, span_len), out_shape=out...  32.9 us
    pallas_call x1, Pallas kernels, shards(): pl.pallas_call(hand_over, out_shape=out_shape, in_specs=[anywhere] * 4, o...  1.78 us

commit v1 on v0

--- a/solution.py
+++ b/solution.py
@@ -24,7 +24,7 @@
     nz, nh, span_len, q_hbm, k_hbm, v_hbm, g_hbm, gain_hbm, kind_hbm, start_hbm, place_hbm,
     o_hbm, dq_hbm, dk_hbm, dv_hbm,
     q_ref, g_ref, gain_ref, kind_ref, start_ref, place_ref, o_ref, dq_ref, dk_ref, dv_ref, in_sems, out_sems,
-    kv, scores, d_probs, tops, k_cols, row_max, row_sum, acc, q_rows, q_cols, g_rows, g_cols, stat, stat_in,
+    kv, scores, d_probs, tops, d_scores_all, k_cols, row_max, row_sum, acc, q_rows, q_cols, g_rows, g_cols, stat, stat_in,
     mine, core_out, core_in, x_out, x_in, z_out, z_in,
     kv_recv, zs_send, xs_send, cs_send, stat_send, stat_recv,
     rc_send, rc_recv, rx_send, rx_recv, rz_send, rz_recv,
@@ -169,7 +169,7 @@
             bias = jnp.where(allowed, 0.0, NEG)
             keys, values = keys_of(j), values_of(j)
             value_cols = values.T
-            k_cols[j] = keys.T
+            k_cols[:, pl.ds(pl.multiple_of(j * pair, pair), pair)] = keys.T
             for group in groups:
                 wide = span_of(group)
                 tile = jnp.dot(keys, q_cols[:, wide], preferred_element_type=F32)
@@ -207,7 +207,6 @@
         for n, (src, dst) in enumerate(((o_ref, o_hbm), (dq_ref, dq_hbm), (dk_ref, dk_hbm), (dv_ref, dv_hbm)))
     ]
     leave[0].start()
-    acc[...] = jnp.zeros(acc.shape, F32)
 
     def core_copy(i):
         return remote(core_out.at[i], core_in.at[i], rc_send.at[i], rc_recv.at[i], core_peer)
@@ -231,21 +230,15 @@
         xx = lax.rem(x + 1 + i // nz, 2)
         j = zz * 2 + xx
         ratio = jnp.exp2(tops[j, 0:1, :] - log_sum)
-        d_key = jnp.zeros((pair, dim), F32)
-        d_value = jnp.zeros((pair, dim), F32)
-        for group in groups:
-            wide = span_of(group)
-            tall = slice(group[0] * tok, (group[-1] + 1) * tok)
-            probs, d_scores = [], []
-            for h in group:
-                c = cols[h]
-                prob = scores[j, :, c] * ratio[:, c]
-                probs.append(prob.astype(BF16))
-                d_scores.append((prob * (d_probs[j, :, c] - deltas[h])).astype(BF16))
-            d_score = jnp.concatenate(d_scores, axis=1)
-            acc[:, wide] += jnp.dot(k_cols[j], d_score, preferred_element_type=F32)
-            d_key += jnp.dot(d_score, q_rows[tall, :], preferred_element_type=F32)
-            d_value += jnp.dot(jnp.concatenate(probs, axis=1), g_rows[tall, :], preferred_element_type=F32)
+        probs, d_scores = [], []
+        for h, c in enumerate(cols):
+            prob = scores[j, :, c] * ratio[:, c]
+            probs.append(prob.astype(BF16))
+            d_scores.append((prob * (d_probs[j, :, c] - deltas[h])).astype(BF16))
+        d_score = jnp.concatenate(d_scores, axis=1)
+        d_scores_all[pl.ds(pl.multiple_of(j * pair, pair), pair), :] = d_score
+        d_key = jnp.dot(d_score, q_rows[...], preferred_element_type=F32)
+        d_value = jnp.dot(jnp.concatenate(probs, axis=1), g_rows[...], preferred_element_type=F32)
         first = core == 0
         for n, grad in enumerate((d_key, d_value)):
             low, high = grad[:tok], grad[tok:]
@@ -258,19 +251,28 @@
             x_out[i - 1] = both_cores(i - 1).astype(BF16)
             x_copy(i - 1).start()
 
-        @pl.when(i > nz)
-        def _():
-            n = i - 1 - nz
-            z_out[n] = both_x(n).astype(BF16)
-            rz_copy(n).start()
-
         return carry
 
     lax.fori_loop(0, steps, backward_step, 0)
 
-    for c in cols:
-        dq_ref[:, c] = acc[:, c].T.astype(BF16)
-    leave[1].start()
+    todo = list(groups)
+
+    def query_group():
+        if not todo:
+            return
+        group = todo.pop(0)
+        grad = jnp.dot(k_cols[...], d_scores_all[:, span_of(group)], preferred_element_type=F32)
+        for n, h in enumerate(group):
+            dq_ref[:, cols[h]] = grad[:, cols[n]].T.astype(BF16)
+        if not todo:
+            leave[1].start()
+
+    for n in range(nz - 1):
+        z_out[n] = both_x(n).astype(BF16)
+        rz_copy(n).start()
+        query_group()
+    while todo:
+        query_group()
     grads = both_x(nz - 1)
     for n in range(nz - 1):
         rz_copy(n).wait_recv()
@@ -352,7 +354,8 @@
                 pltpu.VMEM((steps, 2 * tok, rows), F32),
                 pltpu.VMEM((steps, 2 * tok, rows), F32),
                 pltpu.VMEM((steps, 8, rows), F32),
-                pltpu.VMEM((steps, dim, 2 * tok), BF16),
+                pltpu.VMEM((ranks * tok, rows), BF16),
+                pltpu.VMEM((dim, ranks * tok), BF16),
                 pltpu.VMEM((8, rows), F32),
                 pltpu.VMEM((8, rows), F32),
                 pltpu.VMEM((dim, rows), F32),

time: 35.4 us -> 35.3 us (level)
  no operation moved by 1% of the time
where the time goes in v1:
time: 35.3 us; the launch traced here: 35.2 us
  Pallas kernels  34.5 us (98%)
  between operations  0.64 us (2%)
    pallas_call x1, Pallas kernels, shards(): pl.pallas_call(functools.partial(kernel, nz, nh, span_len), out_shape=out...  32.7 us
    pallas_call x1, Pallas kernels, shards(): pl.pallas_call(hand_over, out_shape=out_shape, in_specs=[anywhere] * 4, o...  1.78 us

profile of v1, /device:TPU:0, one launch (start us, length us, event | category | flops | bytes accessed | tf_op | source)
XLA Modules:
  0.0 35.2 jit_solution(2028791523305656778)
XLA Ops:
  0.6 32.7 %shard_map.111 = (bf16[128,768]{1,0:T(8,128)(2,1)}, bf16[128,768]{1,0:T(8,128)(2,1)}, bf16[128,128]{1,0:T(8,128)(2,1)}, bf16[128,128]{1,0:T(8,128)(2,1)}) custom-call(bf16[128,768]{1,0:T(8,128)(2,1)} %q_hbm.1, bf16[128,128]{1,0:T(8,128)(2,1)} %k_hbm.1, bf16[128,128]{1,0:T(8,128)(2,1)} %v_hbm.1, bf16[128,768]{1,0:T(8,128)(2,1)} %g_hbm.1, f32[768]{0:T(1024)} %gain_hbm.1, ...), custom_call_target="tpu_custom_call" | custom-call | tf_op jit(solution)/shard_map/pallas_call | solution.py:336
  33.4 1.8 %shard_map.112 = (bf16[128,768]{1,0:T(8,128)(2,1)}, bf16[128,768]{1,0:T(8,128)(2,1)}, bf16[128,128]{1,0:T(8,128)(2,1)}, bf16[128,128]{1,0:T(8,128)(2,1)}) custom-call(bf16[128,768]{1,0:T(8,128)(2,1)} %get-tuple-element.8.refs_0_, bf16[128,768]{1,0:T(8,128)(2,1)} %get-tuple-element.9.refs_1_, bf16[128,128]{1,0:T(8,128)(2,1)} %get-tuple-element.10.refs_2_, ...), custom_call_target="tpu_custom_call" | custom-call | tf_op jit(solution)/shard_map/pallas_call | solution.py:387

commit v2 on v1

--- a/solution.py
+++ b/solution.py
@@ -24,7 +24,7 @@
     nz, nh, span_len, q_hbm, k_hbm, v_hbm, g_hbm, gain_hbm, kind_hbm, start_hbm, place_hbm,
     o_hbm, dq_hbm, dk_hbm, dv_hbm,
     q_ref, g_ref, gain_ref, kind_ref, start_ref, place_ref, o_ref, dq_ref, dk_ref, dv_ref, in_sems, out_sems,
-    kv, scores, d_probs, tops, d_scores_all, k_cols, row_max, row_sum, acc, q_rows, q_cols, g_rows, g_cols, stat, stat_in,
+    kv, scores, tops, d_scores_all, k_cols, row_max, row_sum, acc, q_rows, q_cols, g_rows, g_cols, stat, stat_in,
     mine, core_out, core_in, x_out, x_in, z_out, z_in,
     kv_recv, zs_send, xs_send, cs_send, stat_send, stat_recv,
     rc_send, rc_recv, rx_send, rx_recv, rz_send, rz_recv,
@@ -168,28 +168,21 @@
             allowed = k_pos * stride + offset <= q_pos
             bias = jnp.where(allowed, 0.0, NEG)
             keys, values = keys_of(j), values_of(j)
-            value_cols = values.T
-            k_cols[:, pl.ds(pl.multiple_of(j * pair, pair), pair)] = keys.T
-            for group in groups:
-                wide = span_of(group)
-                tile = jnp.dot(keys, q_cols[:, wide], preferred_element_type=F32)
-                d_prob = jnp.dot(values, g_cols[:, wide], preferred_element_type=F32)
-                d_probs[j, :, wide] = d_prob * inv_sqrt
-                weights = []
-                for n, h in enumerate(group):
-                    c = cols[h]
-                    part = tile[:, cols[n]] * scale + bias
-                    old = row_max[0:1, c]
-                    new = jnp.maximum(old, jnp.max(fold_rows(jnp.max, part), axis=0, keepdims=True))
-                    weight = jnp.exp2(part - new)
-                    scores[j, :, c] = weight
-                    factor = jnp.exp2(old - new)
-                    row_max[0:1, c] = new
-                    tops[j, 0:1, c] = new
-                    row_sum[:, c] = row_sum[:, c] * factor + fold_rows(jnp.sum, weight)
-                    acc[:, c] = acc[:, c] * factor
-                    weights.append(weight.astype(BF16))
-                acc[:, wide] += jnp.dot(value_cols, jnp.concatenate(weights, axis=1), preferred_element_type=F32)
+            tile = jnp.dot(keys, q_cols[...], preferred_element_type=F32)
+            weights = []
+            for c in cols:
+                part = tile[:, c] * scale + bias
+                old = row_max[0:1, c]
+                new = jnp.maximum(old, jnp.max(fold_rows(jnp.max, part), axis=0, keepdims=True))
+                weight = jnp.exp2(part - new)
+                scores[j, :, c] = weight
+                factor = jnp.exp2(old - new)
+                row_max[0:1, c] = new
+                tops[j, 0:1, c] = new
+                row_sum[:, c] = row_sum[:, c] * factor + fold_rows(jnp.sum, weight)
+                acc[:, c] = acc[:, c] * factor
+                weights.append(weight.astype(BF16))
+            acc[...] += jnp.dot(values.T, jnp.concatenate(weights, axis=1), preferred_element_type=F32)
 
         return carry
 
@@ -230,11 +223,13 @@
         xx = lax.rem(x + 1 + i // nz, 2)
         j = zz * 2 + xx
         ratio = jnp.exp2(tops[j, 0:1, :] - log_sum)
+        k_cols[:, pl.ds(pl.multiple_of(j * pair, pair), pair)] = keys_of(j).T
+        d_prob = jnp.dot(values_of(j), g_cols[...], preferred_element_type=F32) * inv_sqrt
         probs, d_scores = [], []
         for h, c in enumerate(cols):
             prob = scores[j, :, c] * ratio[:, c]
             probs.append(prob.astype(BF16))
-            d_scores.append((prob * (d_probs[j, :, c] - deltas[h])).astype(BF16))
+            d_scores.append((prob * (d_prob[:, c] - deltas[h])).astype(BF16))
         d_score = jnp.concatenate(d_scores, axis=1)
         d_scores_all[pl.ds(pl.multiple_of(j * pair, pair), pair), :] = d_score
         d_key = jnp.dot(d_score, q_rows[...], preferred_element_type=F32)
@@ -351,7 +346,6 @@
                 pltpu.VMEM((tok, dim), BF16),
                 dma((8,)), dma((4,)),
                 pltpu.VMEM((ranks,) + block, BF16),
-                pltpu.VMEM((steps, 2 * tok, rows), F32),
                 pltpu.VMEM((steps, 2 * tok, rows), F32),
                 pltpu.VMEM((steps, 8, rows), F32),
                 pltpu.VMEM((ranks * tok, rows), BF16),

time: 35.3 us -> 35.1 us (level)
  no operation moved by 1% of the time
where the time goes in v2:
time: 35.1 us; the launch traced here: 34.9 us
  Pallas kernels  34.3 us (98%)
  between operations  0.64 us (2%)
    pallas_call x1, Pallas kernels, shards(): pl.pallas_call(functools.partial(kernel, nz, nh, span_len), out_shape=out...  32.5 us
    pallas_call x1, Pallas kernels, shards(): pl.pallas_call(hand_over, out_shape=out_shape, in_specs=[anywhere] * 4, o...  1.78 us

profile of v2, /device:TPU:0, one launch (start us, length us, event | category | flops | bytes accessed | tf_op | source)
XLA Modules:
  0.0 34.9 jit_solution(12677657091667010563)
XLA Ops:
  0.6 32.5 %shard_map.111 = (bf16[128,768]{1,0:T(8,128)(2,1)}, bf16[128,768]{1,0:T(8,128)(2,1)}, bf16[128,128]{1,0:T(8,128)(2,1)}, bf16[128,128]{1,0:T(8,128)(2,1)}) custom-call(bf16[128,768]{1,0:T(8,128)(2,1)} %q_hbm.1, bf16[128,128]{1,0:T(8,128)(2,1)} %k_hbm.1, bf16[128,128]{1,0:T(8,128)(2,1)} %v_hbm.1, bf16[128,768]{1,0:T(8,128)(2,1)} %g_hbm.1, f32[768]{0:T(1024)} %gain_hbm.1, ...), custom_call_target="tpu_custom_call" | custom-call | tf_op jit(solution)/shard_map/pallas_call | solution.py:331
  33.1 1.8 %shard_map.112 = (bf16[128,768]{1,0:T(8,128)(2,1)}, bf16[128,768]{1,0:T(8,128)(2,1)}, bf16[128,128]{1,0:T(8,128)(2,1)}, bf16[128,128]{1,0:T(8,128)(2,1)}) custom-call(bf16[128,768]{1,0:T(8,128)(2,1)} %get-tuple-element.8.refs_0_, bf16[128,768]{1,0:T(8,128)(2,1)} %get-tuple-element.9.refs_1_, bf16[128,128]{1,0:T(8,128)(2,1)} %get-tuple-element.10.refs_2_, ...), custom_call_target="tpu_custom_call" | custom-call | tf_op jit(solution)/shard_map/pallas_call | solution.py:381

commit v3 on v2

--- a/solution.py
+++ b/solution.py
@@ -68,38 +68,41 @@
     ]
     for move in moves:
         move.start()
-    for move in moves[:3]:
+    for move in moves[:2]:
         move.wait()
+    pl.semaphore_wait(barrier, nz + nh)
+
+    def remote(src, dst, send, recv, ctx_to, head_to=None):
+        return pltpu.make_async_remote_copy(
+            src_ref=src, dst_ref=dst, send_sem=send, recv_sem=recv,
+            device_id=(ctx_to, hd if head_to is None else head_to), device_id_type=MESH,
+        )
+
+    def stat_copy(k):
+        return remote(stat, stat_in.at[k - 1], stat_send.at[k - 1], stat_recv.at[k - 1], me, lax.rem(hd + k, nh))
+
+    def kv_copy(block, send, to):
+        return remote(kv.at[block], kv.at[block], send, kv_recv.at[block], to)
+
+    def shift(i):
+        away = (i + 1) // 2
+        return lax.rem(jnp.where(lax.rem(i, 2) == 1, away, nz - away), nz)
+
+    def z_copy(i):
+        return kv_copy(me, zs_send.at[i - 1], at(lax.rem(z + shift(i), nz), x, core))
+
+    kv_copy(me, xs_send.at[0], x_peer).start()
+    z_copy(1).start()
+    kv_copy(me, cs_send.at[0], core_peer).start()
+    moves[2].wait()
     squares = jnp.zeros((tok, dim), F32)
     for c in cols:
         part = q_ref[:, c].astype(F32)
         squares += part * part
     own_sum = jnp.sum(squares.T, axis=0, keepdims=True)
     stat[...] = jnp.broadcast_to(own_sum, stat.shape)
-    pl.semaphore_wait(barrier, nz + nh)
-
-    def remote(src, dst, send, recv, ctx_to, head_to=None):
-        return pltpu.make_async_remote_copy(
-            src_ref=src, dst_ref=dst, send_sem=send, recv_sem=recv,
-            device_id=(ctx_to, hd if head_to is None else head_to), device_id_type=MESH,
-        )
-
-    def stat_copy(k):
-        return remote(stat, stat_in.at[k - 1], stat_send.at[k - 1], stat_recv.at[k - 1], me, lax.rem(hd + k, nh))
-
-    def kv_copy(block, send, to):
-        return remote(kv.at[block], kv.at[block], send, kv_recv.at[block], to)
-
-    def z_copy(k):
-        return kv_copy(me, zs_send.at[k - 1], at(lax.rem(z + k, nz), x, core))
-
     for k in range(1, nh):
         stat_copy(k).start()
-    kv_copy(me, cs_send.at[0], core_peer).start()
-    kv_copy(me, xs_send.at[0], x_peer).start()
-    for k in range(1, nz):
-        z_copy(k).start()
-
     for move in moves[3:]:
         move.wait()
     for h, c in enumerate(cols):
@@ -109,6 +112,8 @@
     row_max[...] = jnp.full(row_max.shape, NEG, F32)
     row_sum[...] = jnp.zeros(row_sum.shape, F32)
     acc[...] = jnp.zeros(acc.shape, F32)
+    if nz > 2:
+        z_copy(2).start()
     total = own_sum
     for k in range(1, nh):
         stat_copy(k).wait_recv()
@@ -128,7 +133,7 @@
     q_pos = lax.rem(me * tok, span_len) + lax.broadcasted_iota(jnp.int32, (1, tok), 1)
 
     def place_of(i):
-        return lax.rem(z + i, nz), lax.rem(x + i // nz, 2)
+        return lax.rem(z + nz - shift(lax.rem(i, nz)), nz), lax.rem(x + i // nz, 2)
 
     def pair_of(i):
         zz, xx = place_of(i)
@@ -151,6 +156,10 @@
             @pl.when(i < nz)
             def _():
                 kv_copy(block, xs_send.at[i], x_peer).start()
+
+            @pl.when(i < nz - 2)
+            def _():
+                z_copy(i + 2).start()
 
         @pl.when(i > 0)
         def _():

time: 35.1 us -> 34.3 us (0.977)
  Pallas kernels: 34.3 us -> 33.5 us
    pallas_call x1, Pallas kernels: 32.5 us -> 31.7 us  [shards(): pl.pallas_call(functools.partial(kernel, nz, nh, span_len), out_shape=out...]
where the time goes in v3:
time: 34.3 us; the launch traced here: 34.2 us
  Pallas kernels  33.5 us (98%)
  between operations  0.64 us (2%)
    pallas_call x1, Pallas kernels, shards(): pl.pallas_call(functools.partial(kernel, nz, nh, span_len), out_shape=out...  31.7 us
    pallas_call x1, Pallas kernels, shards(): pl.pallas_call(hand_over, out_shape=out_shape, in_specs=[anywhere] * 4, o...  1.78 us

profile of v3, /device:TPU:0, one launch (start us, length us, event | category | flops | bytes accessed | tf_op | source)
XLA Modules:
  0.0 34.2 jit_solution(9772293069320251664)
XLA Ops:
  0.6 31.7 %shard_map.111 = (bf16[128,768]{1,0:T(8,128)(2,1)}, bf16[128,768]{1,0:T(8,128)(2,1)}, bf16[128,128]{1,0:T(8,128)(2,1)}, bf16[128,128]{1,0:T(8,128)(2,1)}) custom-call(bf16[128,768]{1,0:T(8,128)(2,1)} %q_hbm.1, bf16[128,128]{1,0:T(8,128)(2,1)} %k_hbm.1, bf16[128,128]{1,0:T(8,128)(2,1)} %v_hbm.1, bf16[128,768]{1,0:T(8,128)(2,1)} %g_hbm.1, f32[768]{0:T(1024)} %gain_hbm.1, ...), custom_call_target="tpu_custom_call" | custom-call | tf_op jit(solution)/shard_map/pallas_call | solution.py:340
  32.4 1.8 %shard_map.112 = (bf16[128,768]{1,0:T(8,128)(2,1)}, bf16[128,768]{1,0:T(8,128)(2,1)}, bf16[128,128]{1,0:T(8,128)(2,1)}, bf16[128,128]{1,0:T(8,128)(2,1)}) custom-call(bf16[128,768]{1,0:T(8,128)(2,1)} %get-tuple-element.8.refs_0_, bf16[128,768]{1,0:T(8,128)(2,1)} %get-tuple-element.9.refs_1_, bf16[128,128]{1,0:T(8,128)(2,1)} %get-tuple-element.10.refs_2_, ...), custom_call_target="tpu_custom_call" | custom-call | tf_op jit(solution)/shard_map/pallas_call | solution.py:390

commit v4 on v3

--- a/solution.py
+++ b/solution.py
@@ -24,7 +24,7 @@
     nz, nh, span_len, q_hbm, k_hbm, v_hbm, g_hbm, gain_hbm, kind_hbm, start_hbm, place_hbm,
     o_hbm, dq_hbm, dk_hbm, dv_hbm,
     q_ref, g_ref, gain_ref, kind_ref, start_ref, place_ref, o_ref, dq_ref, dk_ref, dv_ref, in_sems, out_sems,
-    kv, scores, tops, d_scores_all, k_cols, row_max, row_sum, acc, q_rows, q_cols, g_rows, g_cols, stat, stat_in,
+    kv, scores, d_probs, tops, d_scores_all, k_cols, row_max, row_sum, acc, q_rows, q_cols, g_rows, g_cols, stat, stat_in,
     mine, core_out, core_in, x_out, x_in, z_out, z_in,
     kv_recv, zs_send, xs_send, cs_send, stat_send, stat_recv,
     rc_send, rc_recv, rx_send, rx_recv, rz_send, rz_recv,
@@ -145,57 +145,82 @@
     def values_of(j):
         return kv[pl.ds(2 * j, 2), 1].reshape(pair, dim)
 
-    def score_step(i, carry):
-        @pl.when((i > 0) & (i < steps))
-        def _():
-            zz, xx = place_of(i)
-            block = at(zz, xx, core)
-            kv_copy(block, cs_send.at[i], core_peer).wait_recv()
-            kv_copy(block, cs_send.at[i], core_peer).start()
-
-            @pl.when(i < nz)
+    def fetch(i):
+        zz, xx = place_of(i)
+        block = at(zz, xx, core)
+        kv_copy(block, cs_send.at[i], core_peer).wait_recv()
+
+        @pl.when(i < nz)
+        def _():
+            kv_copy(block, xs_send.at[i], x_peer).start()
+
+        kv_copy(block, cs_send.at[i], core_peer).start()
+
+        @pl.when(i < nz - 2)
+        def _():
+            z_copy(i + 2).start()
+
+    def bias_of(j):
+        k_slot = (j * pair) // span_len
+        k_span = place_ref[k_slot]
+        before = (lower <= k_span) & (k_span < q_span)
+        own = k_slot == slot
+        stride = jnp.where(own & (causal != 0), 1, 0)
+        offset = jnp.where(own | before, jnp.where(stride == 1, 0, -1), HIDDEN)
+        k_pos = lax.rem(j * pair, span_len) + lax.broadcasted_iota(jnp.int32, (pair, tok), 0)
+        return jnp.where(k_pos * stride + offset <= q_pos, 0.0, NEG)
+
+    def score_step(turn, carry):
+        @pl.when(turn > 0)
+        def _():
+            @pl.when(turn < nz)
             def _():
-                kv_copy(block, xs_send.at[i], x_peer).start()
-
-            @pl.when(i < nz - 2)
-            def _():
-                z_copy(i + 2).start()
-
-        @pl.when(i > 0)
-        def _():
-            zz, xx = place_of(i - 1)
-            j = zz * 2 + xx
-            other = at(zz, xx, 1 - core)
-            kv_copy(other, cs_send.at[0], core_peer).wait_recv()
-            k_slot = (j * pair) // span_len
-            k_span = place_ref[k_slot]
-            before = (lower <= k_span) & (k_span < q_span)
-            own = k_slot == slot
-            stride = jnp.where(own & (causal != 0), 1, 0)
-            offset = jnp.where(own | before, jnp.where(stride == 1, 0, -1), HIDDEN)
-            k_pos = lax.rem(j * pair, span_len) + lax.broadcasted_iota(jnp.int32, (pair, tok), 0)
-            allowed = k_pos * stride + offset <= q_pos
-            bias = jnp.where(allowed, 0.0, NEG)
-            keys, values = keys_of(j), values_of(j)
+                fetch(2 * turn)
+
+        @pl.when(turn < nz)
+        def _():
+            fetch(2 * turn + 1)
+
+        @pl.when(turn > 0)
+        def _():
+            js = []
+            for i in (2 * turn - 2, 2 * turn - 1):
+                zz, xx = place_of(i)
+                kv_copy(at(zz, xx, 1 - core), cs_send.at[0], core_peer).wait_recv()
+                js.append(zz * 2 + xx)
+            biases = [bias_of(j) for j in js]
+            keys = jnp.concatenate([keys_of(j) for j in js], axis=0)
+            values = jnp.concatenate([values_of(j) for j in js], axis=0)
             tile = jnp.dot(keys, q_cols[...], preferred_element_type=F32)
+            d_prob = jnp.dot(values, g_cols[...], preferred_element_type=F32)
+            for n, j in enumerate(js):
+                rows = slice(n * pair, (n + 1) * pair)
+                k_cols[:, pl.ds(pl.multiple_of(j * pair, pair), pair)] = keys[rows].T
+                d_probs[j] = d_prob[rows] * inv_sqrt
             weights = []
             for c in cols:
-                part = tile[:, c] * scale + bias
+                parts = [tile[n * pair:(n + 1) * pair, c] * scale + biases[n] for n in range(2)]
                 old = row_max[0:1, c]
-                new = jnp.maximum(old, jnp.max(fold_rows(jnp.max, part), axis=0, keepdims=True))
-                weight = jnp.exp2(part - new)
-                scores[j, :, c] = weight
+                most = jnp.maximum(fold_rows(jnp.max, parts[0]), fold_rows(jnp.max, parts[1]))
+                new = jnp.maximum(old, jnp.max(most, axis=0, keepdims=True))
                 factor = jnp.exp2(old - new)
                 row_max[0:1, c] = new
-                tops[j, 0:1, c] = new
-                row_sum[:, c] = row_sum[:, c] * factor + fold_rows(jnp.sum, weight)
+                gain = row_sum[:, c] * factor
+                shares = []
+                for j, part in zip(js, parts):
+                    weight = jnp.exp2(part - new)
+                    scores[j, :, c] = weight
+                    tops[j, 0:1, c] = new
+                    gain += fold_rows(jnp.sum, weight)
+                    shares.append(weight.astype(BF16))
+                row_sum[:, c] = gain
                 acc[:, c] = acc[:, c] * factor
-                weights.append(weight.astype(BF16))
+                weights.append(jnp.concatenate(shares, axis=0))
             acc[...] += jnp.dot(values.T, jnp.concatenate(weights, axis=1), preferred_element_type=F32)
 
         return carry
 
-    lax.fori_loop(0, steps + 1, score_step, 0)
+    lax.fori_loop(0, nz + 1, score_step, 0)
 
     sums = jnp.sum(row_sum[...], axis=0, keepdims=True)
     log_sum = row_max[0:1, :] + jnp.log2(sums)
@@ -203,12 +228,11 @@
     for c in cols:
         out = (acc[:, c] / sums[:, c]).astype(BF16).astype(F32)
         deltas.append(jnp.sum(out * g_cols[:, c].astype(F32), axis=0, keepdims=True) * inv_sqrt)
-        o_ref[:, c] = out.T.astype(BF16)
+        acc[:, c] = out
     leave = [
         pltpu.make_async_copy(src, dst, out_sems.at[n])
         for n, (src, dst) in enumerate(((o_ref, o_hbm), (dq_ref, dq_hbm), (dk_ref, dk_hbm), (dv_ref, dv_hbm)))
     ]
-    leave[0].start()
 
     def core_copy(i):
         return remote(core_out.at[i], core_in.at[i], rc_send.at[i], rc_recv.at[i], core_peer)
@@ -232,13 +256,11 @@
         xx = lax.rem(x + 1 + i // nz, 2)
         j = zz * 2 + xx
         ratio = jnp.exp2(tops[j, 0:1, :] - log_sum)
-        k_cols[:, pl.ds(pl.multiple_of(j * pair, pair), pair)] = keys_of(j).T
-        d_prob = jnp.dot(values_of(j), g_cols[...], preferred_element_type=F32) * inv_sqrt
         probs, d_scores = [], []
         for h, c in enumerate(cols):
             prob = scores[j, :, c] * ratio[:, c]
             probs.append(prob.astype(BF16))
-            d_scores.append((prob * (d_prob[:, c] - deltas[h])).astype(BF16))
+            d_scores.append((prob * (d_probs[j, :, c] - deltas[h])).astype(BF16))
         d_score = jnp.concatenate(d_scores, axis=1)
         d_scores_all[pl.ds(pl.multiple_of(j * pair, pair), pair), :] = d_score
         d_key = jnp.dot(d_score, q_rows[...], preferred_element_type=F32)
@@ -259,6 +281,9 @@
 
     lax.fori_loop(0, steps, backward_step, 0)
 
+    for c in cols:
+        o_ref[:, c] = acc[:, c].T.astype(BF16)
+    leave[0].start()
     todo = list(groups)
 
     def query_group():
@@ -355,6 +380,7 @@
                 pltpu.VMEM((tok, dim), BF16),
                 dma((8,)), dma((4,)),
                 pltpu.VMEM((ranks,) + block, BF16),
+                pltpu.VMEM((steps, 2 * tok, rows), F32),
                 pltpu.VMEM((steps, 2 * tok, rows), F32),
                 pltpu.VMEM((steps, 8, rows), F32),
                 pltpu.VMEM((ranks * tok, rows), BF16),

time: 34.3 us -> 33.9 us (0.988)
  Pallas kernels: 33.5 us -> 33.1 us
    pallas_call x1, Pallas kernels: 31.7 us -> 31.3 us  [shards(): pl.pallas_call(functools.partial(kernel, nz, nh, span_len), out_shape=out...]
where the time goes in v4:
time: 33.9 us; the launch traced here: 33.7 us
  Pallas kernels  33.1 us (98%)
  between operations  0.64 us (2%)
    pallas_call x1, Pallas kernels, shards(): pl.pallas_call(functools.partial(kernel, nz, nh, span_len), out_shape=out...  31.3 us
    pallas_call x1, Pallas kernels, shards(): pl.pallas_call(hand_over, out_shape=out_shape, in_specs=[anywhere] * 4, o...  1.78 us

profile of v4, /device:TPU:0, one launch (start us, length us, event | category | flops | bytes accessed | tf_op | source)
XLA Modules:
  0.0 33.7 jit_solution(17766481068673303263)
XLA Ops:
  0.6 31.3 %shard_map.111 = (bf16[128,768]{1,0:T(8,128)(2,1)}, bf16[128,768]{1,0:T(8,128)(2,1)}, bf16[128,128]{1,0:T(8,128)(2,1)}, bf16[128,128]{1,0:T(8,128)(2,1)}) custom-call(bf16[128,768]{1,0:T(8,128)(2,1)} %q_hbm.1, bf16[128,128]{1,0:T(8,128)(2,1)} %k_hbm.1, bf16[128,128]{1,0:T(8,128)(2,1)} %v_hbm.1, bf16[128,768]{1,0:T(8,128)(2,1)} %g_hbm.1, f32[768]{0:T(1024)} %gain_hbm.1, ...), custom_call_target="tpu_custom_call" | custom-call | tf_op jit(solution)/shard_map/pallas_call | solution.py:365
  32.0 1.8 %shard_map.112 = (bf16[128,768]{1,0:T(8,128)(2,1)}, bf16[128,768]{1,0:T(8,128)(2,1)}, bf16[128,128]{1,0:T(8,128)(2,1)}, bf16[128,128]{1,0:T(8,128)(2,1)}) custom-call(bf16[128,768]{1,0:T(8,128)(2,1)} %get-tuple-element.8.refs_0_, bf16[128,768]{1,0:T(8,128)(2,1)} %get-tuple-element.9.refs_1_, bf16[128,128]{1,0:T(8,128)(2,1)} %get-tuple-element.10.refs_2_, ...), custom_call_target="tpu_custom_call" | custom-call | tf_op jit(solution)/shard_map/pallas_call | solution.py:416

commit v5 on v4

--- a/solution.py
+++ b/solution.py
@@ -251,7 +251,13 @@
         x_copy(i).wait_recv()
         return both_cores(nz + i) + x_in[i].astype(F32)
 
-    def backward_step(i, carry):
+    def place_in_order(i):
+        last = i == steps - 1
+        crossing = (i < 2) | ((lax.rem(i, 2) == 1) & (i < steps - 1))
+        return jnp.where(crossing, (i + 1) // 2, jnp.where(last, steps - 1, nz + i // 2 - 1))
+
+    def backward_step(turn, carry):
+        i = place_in_order(turn)
         zz = lax.rem(z + 1 + i, nz)
         xx = lax.rem(x + 1 + i // nz, 2)
         j = zz * 2 + xx
@@ -272,10 +278,18 @@
             core_out[i, n] = jnp.where(first, high, low).astype(BF16)
         core_copy(i).start()
 
-        @pl.when((i >= 1) & (i <= nz))
-        def _():
-            x_out[i - 1] = both_cores(i - 1).astype(BF16)
-            x_copy(i - 1).start()
+        done = place_in_order(jnp.maximum(turn - 1, 0))
+
+        @pl.when((turn > 0) & (done < nz))
+        def _():
+            x_out[done] = both_cores(done).astype(BF16)
+            x_copy(done).start()
+
+        @pl.when((turn > 0) & (done >= nz))
+        def _():
+            n = done - nz
+            z_out[n] = both_x(n).astype(BF16)
+            rz_copy(n).start()
 
         return carry
 
@@ -296,10 +310,6 @@
         if not todo:
             leave[1].start()
 
-    for n in range(nz - 1):
-        z_out[n] = both_x(n).astype(BF16)
-        rz_copy(n).start()
-        query_group()
     while todo:
         query_group()
     grads = both_x(nz - 1)

time: 33.9 us -> 34.6 us (1.021)
  Pallas kernels: 33.1 us -> 33.8 us
    pallas_call x1, Pallas kernels: 31.3 us -> 32 us  [shards(): pl.pallas_call(functools.partial(kernel, nz, nh, span_len), out_shape=out...]
where the time goes in v5:
time: 34.6 us; the launch traced here: 34.5 us
  Pallas kernels  33.8 us (98%)
  between operations  0.64 us (2%)
    pallas_call x1, Pallas kernels, shards(): pl.pallas_call(functools.partial(kernel, nz, nh, span_len), out_shape=out...  32 us
    pallas_call x1, Pallas kernels, shards(): pl.pallas_call(hand_over, out_shape=out_shape, in_specs=[anywhere] * 4, o...  1.78 us

profile of v5, /device:TPU:0, one launch (start us, length us, event | category | flops | bytes accessed | tf_op | source)
XLA Modules:
  0.0 34.5 jit_solution(11944977267446824795)
XLA Ops:
  0.6 32.0 %shard_map.111 = (bf16[128,768]{1,0:T(8,128)(2,1)}, bf16[128,768]{1,0:T(8,128)(2,1)}, bf16[128,128]{1,0:T(8,128)(2,1)}, bf16[128,128]{1,0:T(8,128)(2,1)}) custom-call(bf16[128,768]{1,0:T(8,128)(2,1)} %q_hbm.1, bf16[128,128]{1,0:T(8,128)(2,1)} %k_hbm.1, bf16[128,128]{1,0:T(8,128)(2,1)} %v_hbm.1, bf16[128,768]{1,0:T(8,128)(2,1)} %g_hbm.1, f32[768]{0:T(1024)} %gain_hbm.1, ...), custom_call_target="tpu_custom_call" | custom-call | tf_op jit(solution)/shard_map/pallas_call | solution.py:375
  32.7 1.8 %shard_map.112 = (bf16[128,768]{1,0:T(8,128)(2,1)}, bf16[128,768]{1,0:T(8,128)(2,1)}, bf16[128,128]{1,0:T(8,128)(2,1)}, bf16[128,128]{1,0:T(8,128)(2,1)}) custom-call(bf16[128,768]{1,0:T(8,128)(2,1)} %get-tuple-element.8.refs_0_, bf16[128,768]{1,0:T(8,128)(2,1)} %get-tuple-element.9.refs_1_, bf16[128,128]{1,0:T(8,128)(2,1)} %get-tuple-element.10.refs_2_, ...), custom_call_target="tpu_custom_call" | custom-call | tf_op jit(solution)/shard_map/pallas_call | solution.py:426

commit v6 on v4

--- a/solution.py
+++ b/solution.py
@@ -277,6 +277,12 @@
             x_out[i - 1] = both_cores(i - 1).astype(BF16)
             x_copy(i - 1).start()
 
+        @pl.when(i > nz)
+        def _():
+            n = i - 1 - nz
+            z_out[n] = both_x(n).astype(BF16)
+            rz_copy(n).start()
+
         return carry
 
     lax.fori_loop(0, steps, backward_step, 0)
@@ -296,10 +302,6 @@
         if not todo:
             leave[1].start()
 
-    for n in range(nz - 1):
-        z_out[n] = both_x(n).astype(BF16)
-        rz_copy(n).start()
-        query_group()
     while todo:
         query_group()
     grads = both_x(nz - 1)

time: 33.9 us -> 33.9 us (level)
  no operation moved by 1% of the time
where the time goes in v6:
time: 33.9 us; the launch traced here: 33.7 us
  Pallas kernels  33.1 us (98%)
  between operations  0.64 us (2%)
    pallas_call x1, Pallas kernels, shards(): pl.pallas_call(functools.partial(kernel, nz, nh, span_len), out_shape=out...  31.3 us
    pallas_call x1, Pallas kernels, shards(): pl.pallas_call(hand_over, out_shape=out_shape, in_specs=[anywhere] * 4, o...  1.78 us

profile of v6, /device:TPU:0, one launch (start us, length us, event | category | flops | bytes accessed | tf_op | source)
XLA Modules:
  0.0 33.7 jit_solution(9663519314490700836)
XLA Ops:
  0.6 31.3 %shard_map.111 = (bf16[128,768]{1,0:T(8,128)(2,1)}, bf16[128,768]{1,0:T(8,128)(2,1)}, bf16[128,128]{1,0:T(8,128)(2,1)}, bf16[128,128]{1,0:T(8,128)(2,1)}) custom-call(bf16[128,768]{1,0:T(8,128)(2,1)} %q_hbm.1, bf16[128,128]{1,0:T(8,128)(2,1)} %k_hbm.1, bf16[128,128]{1,0:T(8,128)(2,1)} %v_hbm.1, bf16[128,768]{1,0:T(8,128)(2,1)} %g_hbm.1, f32[768]{0:T(1024)} %gain_hbm.1, ...), custom_call_target="tpu_custom_call" | custom-call | tf_op jit(solution)/shard_map/pallas_call | solution.py:367
  31.9 1.8 %shard_map.112 = (bf16[128,768]{1,0:T(8,128)(2,1)}, bf16[128,768]{1,0:T(8,128)(2,1)}, bf16[128,128]{1,0:T(8,128)(2,1)}, bf16[128,128]{1,0:T(8,128)(2,1)}) custom-call(bf16[128,768]{1,0:T(8,128)(2,1)} %get-tuple-element.8.refs_0_, bf16[128,768]{1,0:T(8,128)(2,1)} %get-tuple-element.9.refs_1_, bf16[128,128]{1,0:T(8,128)(2,1)} %get-tuple-element.10.refs_2_, ...), custom_call_target="tpu_custom_call" | custom-call | tf_op jit(solution)/shard_map/pallas_call | solution.py:418

commit v7 on v6

--- a/solution.py
+++ b/solution.py
@@ -177,10 +177,6 @@
             def _():
                 fetch(2 * turn)
 
-        @pl.when(turn < nz)
-        def _():
-            fetch(2 * turn + 1)
-
         @pl.when(turn > 0)
         def _():
             js = []
@@ -217,6 +213,10 @@
                 acc[:, c] = acc[:, c] * factor
                 weights.append(jnp.concatenate(shares, axis=0))
             acc[...] += jnp.dot(values.T, jnp.concatenate(weights, axis=1), preferred_element_type=F32)
+
+        @pl.when(turn < nz)
+        def _():
+            fetch(2 * turn + 1)
 
         return carry
 

time: 33.9 us -> 34.5 us (1.018)
  Pallas kernels: 33.1 us -> 33.7 us
    pallas_call x1, Pallas kernels: 31.3 us -> 32 us  [shards(): pl.pallas_call(functools.partial(kernel, nz, nh, span_len), out_shape=out...]
where the time goes in v7:
time: 34.5 us; the launch traced here: 34.4 us
  Pallas kernels  33.7 us (98%)
  between operations  0.64 us (2%)
    pallas_call x1, Pallas kernels, shards(): pl.pallas_call(functools.partial(kernel, nz, nh, span_len), out_shape=out...  32 us
    pallas_call x1, Pallas kernels, shards(): pl.pallas_call(hand_over, out_shape=out_shape, in_specs=[anywhere] * 4, o...  1.78 us

profile of v7, /device:TPU:0, one launch (start us, length us, event | category | flops | bytes accessed | tf_op | source)
XLA Modules:
  0.0 34.4 jit_solution(83470733015494979)
XLA Ops:
  0.6 32.0 %shard_map.111 = (bf16[128,768]{1,0:T(8,128)(2,1)}, bf16[128,768]{1,0:T(8,128)(2,1)}, bf16[128,128]{1,0:T(8,128)(2,1)}, bf16[128,128]{1,0:T(8,128)(2,1)}) custom-call(bf16[128,768]{1,0:T(8,128)(2,1)} %q_hbm.1, bf16[128,128]{1,0:T(8,128)(2,1)} %k_hbm.1, bf16[128,128]{1,0:T(8,128)(2,1)} %v_hbm.1, bf16[128,768]{1,0:T(8,128)(2,1)} %g_hbm.1, f32[768]{0:T(1024)} %gain_hbm.1, ...), custom_call_target="tpu_custom_call" | custom-call | tf_op jit(solution)/shard_map/pallas_call | solution.py:367
  32.6 1.8 %shard_map.112 = (bf16[128,768]{1,0:T(8,128)(2,1)}, bf16[128,768]{1,0:T(8,128)(2,1)}, bf16[128,128]{1,0:T(8,128)(2,1)}, bf16[128,128]{1,0:T(8,128)(2,1)}) custom-call(bf16[128,768]{1,0:T(8,128)(2,1)} %get-tuple-element.8.refs_0_, bf16[128,768]{1,0:T(8,128)(2,1)} %get-tuple-element.9.refs_1_, bf16[128,128]{1,0:T(8,128)(2,1)} %get-tuple-element.10.refs_2_, ...), custom_call_target="tpu_custom_call" | custom-call | tf_op jit(solution)/shard_map/pallas_call | solution.py:418
